TPU v7x, 32 devices: a whole 2x2x4 slice. The times are simulated.
32 devices in a mesh: ctx: 4 (over x, core), fsdp: 8 (over z, y).
Axes of the slice: x: 2, y: 2, z: 4, core: 2. Of those that a mesh axis runs over, the one named last changes fastest.
Arguments:
- inputs: bfloat16 [8, 512, 2048], P('fsdp', 'ctx'), may hold values from -6 to 6
- doc_starts: int32 [8, 512], P('fsdp'), may hold values from 0 to 1, as said below
- routes: int32 [8, 512, 8], P('fsdp', 'ctx'), may hold values from 0 to 23, all different within a row; in each aligned block of 128 rows (0 to 127, 128 to 255, ..., all dimensions but the last counted through in order) at most 53 rows name the same one
- gate_weights: float32 [8, 512, 8], P('fsdp', 'ctx'), may hold values from 0.04 to 0.25
- qkv_w: bfloat16 [2048, 3, 2048], P('fsdp'), may hold values from -0.125 to 0.125
- out_w: bfloat16 [2048, 2048], P('fsdp'), may hold values from -2 to 2
- norm_gains: bfloat16 [2048, 2], P('fsdp'), may hold values from 0.5 to 1.5
- head_gains: bfloat16 [128, 2], P('fsdp'), may hold values from 0.5 to 1.5
- gate_up: bfloat16 [2048, 24, 2048], P('ctx', 'fsdp'), may hold values from -0.125 to 0.125
- down_t: bfloat16 [2048, 24, 1024], P('ctx', 'fsdp'), may hold values from -0.75 to 0.75
- cotangent: bfloat16 [8, 512, 2048], P('fsdp', 'ctx'), may hold values from -6 to 6
Outputs:
- block_out: bfloat16 [8, 512, 2048], P('fsdp', 'ctx')
- inputs_grad: float32 [8, 512, 2048], P('fsdp', 'ctx')
- qkv_w_grad: float32 [2048, 3, 2048], P('fsdp')
- out_w_grad: float32 [2048, 2048], P('fsdp')
- norm_gains_grad: float32 [2048, 2], P('fsdp')
- head_gains_grad: float32 [128, 2], P('fsdp')
- gate_up_grad: float32 [2048, 24, 2048], P('ctx', 'fsdp')
- down_t_grad: float32 [2048, 24, 1024], P('ctx', 'fsdp')
Inputs may be any that keep to these rules, and one draw needn't show every extreme that they name: `doc_starts`: 1 marks the first position of a document; position 0 of every stream is 1. `routes`: each row names 8 different experts; in the rows of one device no expert is named more than 53 times, a bound that some block reaches.
All inputs are finite; a program needn't handle non-finite values.
Results may differ from a plain program's by a relative error of at most 0.02.
Values may be sent and summed in bfloat16 or wider, within the bound.
No kernel may reach another device: no remote copies, remote signals or barrier semaphores. Data moves between devices by JAX's collectives and lax.ppermute only.
A program may use at most 384 MiB of HBM per device.

v0:
```python
import math
import jax
import jax.numpy as jnp
from jax import lax
from jax.sharding import PartitionSpec as P

EPS = 1e-06
ROPE_BASE = 10000.0
NEG_FILL = -1e30


def rms_scale(values, gain):
    return values * lax.rsqrt(jnp.mean(values * values, axis=-1, keepdims=True) + EPS) * gain


def rotate(values, cosine, sine_part):
    half_dim = values.shape[-1] // 2
    first = values[..., :half_dim]
    second = values[..., half_dim:]
    return jnp.concatenate(
        [first * cosine - second * sine_part, second * cosine + first * sine_part], axis=-1
    )


def body(
    inputs,
    doc_starts,
    routes,
    gate_weights,
    qkv_w,
    out_w,
    norm_gains,
    head_gains,
    gate_up,
    down_t,
    cotangent,
):
    tok_rows = inputs.shape[1]
    model_width = inputs.shape[2]
    head_dim = head_gains.shape[0] * lax.axis_size("fsdp")
    head_count = model_width // head_dim
    half_dim = head_dim // 2
    score_scale = head_dim ** (-0.5)
    top_count = routes.shape[2]
    hidden_units = down_t.shape[2]
    local_experts = gate_up.shape[1]
    experts_all = local_experts * lax.axis_size("fsdp")
    capacity = tok_rows * top_count * 5 // (experts_all * 4)
    stream_len = doc_starts.shape[1]
    key_width = min(512, stream_len)
    key_count = stream_len // key_width
    position = lax.axis_index("ctx") * tok_rows
    f32 = jnp.float32
    bf16 = jnp.bfloat16
    places = jnp.arange(stream_len, dtype=jnp.int32)
    starts = doc_starts[0]
    begins = lax.cummax(jnp.where(starts == 1, places, jnp.zeros_like(places)), axis=0)
    doc_ids = jnp.cumsum(starts)
    relative = places - begins
    local_docs = lax.dynamic_slice_in_dim(doc_ids, position, tok_rows)
    local_rel = lax.dynamic_slice_in_dim(relative, position, tok_rows)
    key_docs = doc_ids.reshape(key_count, key_width)
    frequency = jnp.exp(jnp.arange(half_dim, dtype=f32) * (-2.0 / head_dim) * math.log(ROPE_BASE))
    angles = local_rel.astype(f32)[:, None] * frequency[None, :]
    cosine = jnp.cos(angles)[:, None, :]
    sine_part = jnp.sin(angles)[:, None, :]
    qkv_full, out_full, norm_full, head_full = (
        lax.all_gather(qkv_w, "fsdp", axis=0, tiled=True),
        lax.all_gather(out_w, "fsdp", axis=0, tiled=True),
        lax.all_gather(norm_gains, "fsdp", axis=0, tiled=True),
        lax.all_gather(head_gains, "fsdp", axis=0, tiled=True),
    )
    x_rows = inputs[0].astype(f32)
    cot_rows = cotangent[0].astype(f32)
    a1_f32, norm_one_back = jax.vjp(rms_scale, x_rows, norm_full[:, 0].astype(f32))
    a1_low = a1_f32.astype(bf16)
    proj = jnp.einsum("td,djk->tjk", a1_low, qkv_full, preferred_element_type=f32)

    def prepare(q_flat, k_flat, q_gain, k_gain):
        q_heads = rms_scale(q_flat.reshape(tok_rows, head_count, head_dim), q_gain)
        k_heads = rms_scale(k_flat.reshape(tok_rows, head_count, head_dim), k_gain)
        return (rotate(q_heads, cosine, sine_part), rotate(k_heads, cosine, sine_part))

    (q_rot, k_rot), prepare_back = jax.vjp(
        prepare, proj[:, 0], proj[:, 1], head_full[:, 0].astype(f32), head_full[:, 1].astype(f32)
    )
    q_low = q_rot.astype(bf16)
    k_low = k_rot.reshape(tok_rows, model_width).astype(bf16)
    v_low = proj[:, 2].astype(bf16)
    keys_all, values_all = (
        lax.all_gather(k_low, "ctx", axis=0, tiled=True),
        lax.all_gather(v_low, "ctx", axis=0, tiled=True),
    )
    key_blocks = keys_all.reshape(key_count, key_width, head_count, head_dim)
    value_blocks = values_all.reshape(key_count, key_width, head_count, head_dim)

    def block_logits(key_block, doc_block):
        logits = (
            jnp.einsum("qhd,khd->hqk", q_low, key_block, preferred_element_type=f32) * score_scale
        )
        same_doc = (local_docs[:, None] == doc_block[None, :])[None]
        return jnp.where(same_doc, logits, NEG_FILL)

    def max_step(running, pieces):
        row_max, summed = running
        key_block, doc_block = pieces
        logits = block_logits(key_block, doc_block)
        new_max = jnp.maximum(row_max, jnp.max(logits, axis=2))
        summed = summed * jnp.exp(row_max - new_max) + jnp.sum(
            jnp.exp(logits - new_max[:, :, None]), axis=2
        )
        return ((new_max, summed), None)

    start_max = jnp.full((head_count, tok_rows), NEG_FILL, f32)
    (row_max, summed), _ = lax.scan(
        max_step, (start_max, jnp.zeros((head_count, tok_rows), f32)), (key_blocks, key_docs)
    )
    log_total = row_max + jnp.log(summed)

    def value_step(attn_acc, pieces):
        key_block, value_block, doc_block = pieces
        attn_probs = jnp.exp(block_logits(key_block, doc_block) - log_total[:, :, None])
        return (
            attn_acc
            + jnp.einsum(
                "hqk,khd->qhd", attn_probs.astype(bf16), value_block, preferred_element_type=f32
            ),
            None,
        )

    attn_acc, _ = lax.scan(
        value_step,
        jnp.zeros((tok_rows, head_count, head_dim), f32),
        (key_blocks, value_blocks, key_docs),
    )
    attn_low = attn_acc.reshape(tok_rows, model_width).astype(bf16)
    h_one = x_rows + jnp.dot(attn_low, out_full, preferred_element_type=f32)
    a2_f32, norm_two_back = jax.vjp(rms_scale, h_one, norm_full[:, 1].astype(f32))
    a2_low = a2_f32.astype(bf16)
    flat_routes = routes[0].reshape(tok_rows * top_count)
    onehot = (flat_routes[:, None] == jnp.arange(experts_all, dtype=jnp.int32)[None, :]).astype(
        jnp.int32
    )
    earlier = jnp.cumsum(onehot, axis=0) - onehot
    slot_in = jnp.sum(earlier * onehot, axis=1)
    slot_index = flat_routes * capacity + slot_in
    token_of = jnp.arange(tok_rows * top_count, dtype=jnp.int32) // top_count
    send_rows = (
        jnp.zeros((experts_all * capacity, model_width), bf16).at[slot_index].set(a2_low[token_of])
    )
    scaled = (
        (gate_weights[0][:, :, None] * cot_rows[:, None, :])
        .reshape(tok_rows * top_count, model_width)
        .astype(bf16)
    )
    send_grads = jnp.zeros((experts_all * capacity, model_width), bf16).at[slot_index].set(scaled)
    got_rows, got_grads = (
        lax.all_to_all(
            send_rows.reshape(experts_all, capacity, model_width),
            "fsdp",
            split_axis=0,
            concat_axis=1,
            tiled=True,
        ),
        lax.all_to_all(
            send_grads.reshape(experts_all, capacity, model_width),
            "fsdp",
            split_axis=0,
            concat_axis=1,
            tiled=True,
        ),
    )
    segment = lax.all_gather(gate_up, "ctx", axis=0, tiled=True)
    gate_add = jnp.einsum(
        "erd,dek->erk", got_rows, segment[:, :, :hidden_units], preferred_element_type=f32
    )
    up_add = jnp.einsum(
        "erd,dek->erk", got_rows, segment[:, :, hidden_units:], preferred_element_type=f32
    )
    sigmoid_g = jax.nn.sigmoid(gate_add)
    activated = gate_add * sigmoid_g
    hidden_low = (activated * up_add).astype(bf16)
    segment = lax.all_gather(down_t, "ctx", axis=0, tiled=True)
    made_block = jnp.einsum("erf,def->erd", hidden_low, segment, preferred_element_type=f32).astype(
        bf16
    )
    made_rows = made_block
    hidden_grad = jnp.einsum("erd,def->erf", got_grads, segment, preferred_element_type=f32)
    made_rows, hidden_grad = (made_rows, hidden_grad)
    gate_grad_low = (
        hidden_grad * up_add * sigmoid_g * (1.0 + gate_add * (1.0 - sigmoid_g))
    ).astype(bf16)
    up_grad_low = (hidden_grad * activated).astype(bf16)
    segment = lax.all_gather(gate_up, "ctx", axis=0, tiled=True)
    part_gate = jnp.einsum(
        "erk,dek->erd", gate_grad_low, segment[:, :, :hidden_units], preferred_element_type=f32
    )
    part_up = jnp.einsum(
        "erk,dek->erd", up_grad_low, segment[:, :, hidden_units:], preferred_element_type=f32
    )
    input_grads = (part_gate + part_up).astype(bf16)
    expert_sums = lax.psum_scatter(
        jnp.concatenate(
            [
                jnp.einsum("erd,erk->dek", got_rows, gate_grad_low, preferred_element_type=f32),
                jnp.einsum("erd,erk->dek", got_rows, up_grad_low, preferred_element_type=f32),
                jnp.einsum("erd,erf->def", got_grads, hidden_low, preferred_element_type=f32),
            ],
            axis=2,
        ).astype(jnp.bfloat16),
        "ctx",
        scatter_dimension=0,
        tiled=True,
    ).astype(jnp.float32)
    back_out, back_in = (
        lax.all_to_all(made_rows, "fsdp", split_axis=1, concat_axis=0, tiled=True),
        lax.all_to_all(input_grads, "fsdp", split_axis=1, concat_axis=0, tiled=True),
    )
    out_rows = back_out.reshape(experts_all * capacity, model_width)[slot_index].reshape(
        tok_rows, top_count, model_width
    )
    mixed = jnp.sum(gate_weights[0][:, :, None] * out_rows.astype(f32), axis=1)
    block_out = (h_one + mixed).astype(bf16)
    in_rows = back_in.reshape(experts_all * capacity, model_width)[slot_index].reshape(
        tok_rows, top_count, model_width
    )
    da2 = jnp.sum(in_rows.astype(f32), axis=1)
    dh_part, gain_two_grad = norm_two_back(da2)
    dh_one = cot_rows + dh_part
    dattn = dh_one.astype(bf16)
    out_grad_low = (
        jnp.einsum("tk,dk->td", dattn, out_full, preferred_element_type=f32)
        .astype(bf16)
        .reshape(tok_rows, head_count, head_dim)
    )
    row_delta = jnp.einsum("qhd,qhd->hq", out_grad_low.astype(f32), attn_acc)

    def grad_step(query_grad, pieces):
        key_block, value_block, doc_block = pieces
        attn_probs = jnp.exp(block_logits(key_block, doc_block) - log_total[:, :, None])
        prob_grad = jnp.einsum(
            "qhd,khd->hqk", out_grad_low, value_block, preferred_element_type=f32
        )
        logit_grad = (attn_probs * (prob_grad - row_delta[:, :, None])).astype(bf16)
        query_grad = (
            query_grad
            + jnp.einsum("hqk,khd->qhd", logit_grad, key_block, preferred_element_type=f32)
            * score_scale
        )
        key_grad = (
            jnp.einsum("hqk,qhd->khd", logit_grad, q_low, preferred_element_type=f32) * score_scale
        )
        value_grad = jnp.einsum(
            "hqk,qhd->khd", attn_probs.astype(bf16), out_grad_low, preferred_element_type=f32
        )
        return (query_grad, (key_grad, value_grad))

    query_grad, (key_grads, value_grads) = lax.scan(
        grad_step,
        jnp.zeros((tok_rows, head_count, head_dim), f32),
        (key_blocks, value_blocks, key_docs),
    )
    key_sum, value_sum = (
        lax.psum_scatter(
            key_grads.reshape(stream_len, model_width).astype(jnp.bfloat16),
            "ctx",
            scatter_dimension=0,
            tiled=True,
        ).astype(jnp.float32),
        lax.psum_scatter(
            value_grads.reshape(stream_len, model_width).astype(jnp.bfloat16),
            "ctx",
            scatter_dimension=0,
            tiled=True,
        ).astype(jnp.float32),
    )
    key_low = key_sum.astype(bf16).astype(f32).reshape(tok_rows, head_count, head_dim)
    query_low = query_grad.astype(bf16).astype(f32)
    dq_proj, dk_proj, q_gain_grad, k_gain_grad = prepare_back((query_low, key_low))
    proj_grad = jnp.stack([dq_proj, dk_proj, value_sum], axis=1).astype(bf16)
    da1 = jnp.einsum("tjk,djk->td", proj_grad, qkv_full, preferred_element_type=f32)
    dx_part, gain_one_grad = norm_one_back(da1)
    inputs_grad = dh_one + dx_part
    projections = jnp.einsum("td,tjk->djk", a1_low, proj_grad, preferred_element_type=f32)
    output_part = jnp.einsum("td,tk->dk", attn_low, dattn, preferred_element_type=f32)
    attn_shard = lax.psum_scatter(
        jnp.concatenate([projections, output_part[:, None, :]], axis=1).astype(jnp.bfloat16),
        "fsdp",
        scatter_dimension=0,
        tiled=True,
    )
    norm_part = jnp.stack([gain_one_grad, gain_two_grad], axis=1)
    head_part = jnp.stack([q_gain_grad, k_gain_grad], axis=1)
    norm_shard, head_shard = (
        lax.psum_scatter(norm_part, "fsdp", scatter_dimension=0, tiled=True),
        lax.psum_scatter(head_part, "fsdp", scatter_dimension=0, tiled=True),
    )
    totals = (
        lax.psum(attn_shard, "ctx").astype(jnp.float32),
        lax.psum(norm_shard.astype(jnp.bfloat16), "ctx").astype(jnp.float32),
        lax.psum(head_shard.astype(jnp.bfloat16), "ctx").astype(jnp.float32),
    )
    return (
        block_out[None],
        inputs_grad[None],
        totals[0][:, :3, :],
        totals[0][:, 3, :],
        totals[1],
        totals[2],
        expert_sums[:, :, : 2 * hidden_units],
        expert_sums[:, :, 2 * hidden_units :],
    )


def solution(mesh):
    return jax.shard_map(
        body,
        mesh=mesh,
        in_specs=(
            P("fsdp", "ctx", None),
            P("fsdp", None),
            P("fsdp", "ctx", None),
            P("fsdp", "ctx", None),
            P("fsdp", None, None),
            P("fsdp", None),
            P("fsdp", None),
            P("fsdp", None),
            P("ctx", "fsdp", None),
            P("ctx", "fsdp", None),
            P("fsdp", "ctx", None),
        ),
        out_specs=(
            P("fsdp", "ctx", None),
            P("fsdp", "ctx", None),
            P("fsdp", None, None),
            P("fsdp", None),
            P("fsdp", None),
            P("fsdp", None),
            P("ctx", "fsdp", None),
            P("ctx", "fsdp", None),
        ),
        check_vma=False,
    )
```

profile of v0, /device:TPU:0, one launch (start us, length us, event | category | flops | bytes accessed | tf_op | source)
XLA Modules:
  0.0 2599.0 jit_solution(13533799499513804395)
XLA Ops:
  7.9 50.7 %all_gather.25 = bf16[2048,2]{0,1:T(2,128)(2,1)S(1)} all-gather(bf16[256,2]{0,1:T(2,128)(2,1)} %param.17), channel_id=1, replica_groups=mesh['ctx'=4,'fsdp'=8] {'fsdp'}, dimensions={0}, use_global_device_ids=true | all-gather | bytes 9216 | tf_op jit(solution)/shard_map/all_gather | solution.py:70
  60.5 432.3 %all-gather.9.cloned.1.call-done = bf16[2048,3,2048]{2,0,1:T(8,128)(2,1)} async-done(((bf16[256,3,2048]{2,0,1:T(8,128)(2,1)}), bf16[2048,3,2048]{2,0,1:T(8,128)(2,1)}) %all-gather.9.cloned.1.call-update) | async-done | bytes 25165840 | tf_op jit(solution)/shard_map/all_gather | solution.py:68
  492.8 10.3 fusion.52
  504.5 19.2 all-gather.1
  533.5 6.8 reduce-window.36
  540.9 10.2 scatter_custom_fusion.1
  551.1 6.5 reshape.418
  557.6 4.7 all-to-all-start.2
  575.0 207.0 %all-gather.13.cloned.1.call-done = bf16[2048,2048]{1,0:T(8,128)(2,1)} async-done(((bf16[256,2048]{1,0:T(8,128)(2,1)}), bf16[2048,2048]{1,0:T(8,128)(2,1)}) %all-gather.13.cloned.1.call-update) | async-done | bytes 8388624 | tf_op jit(solution)/shard_map/all_gather | solution.py:69
  782.0 4.7 multiply_reduce_fusion.6
  787.9 23.4 scatter_custom_fusion
  811.3 7.0 reshape.416
  818.3 4.7 all-to-all-start
  823.0 5.9 copy.184
  828.9 6.6 all_to_all.58
  835.5 29.1 %all-gather.17.cloned.1.call-done = bf16[2048,3,1024]{2,0,1:T(8,128)(2,1)} async-done(((bf16[512,3,1024]{2,0,1:T(8,128)(2,1)}), bf16[2048,3,1024]{2,0,1:T(8,128)(2,1)}) %all-gather.17.cloned.1.call-update) | async-done | bytes 12582928 | tf_op jit(solution)/shard_map/all_gather | solution.py:183
  864.6 11.8 fusion.69
  876.4 68.4 %all-to-all-done = bf16[24,53,2048]{2,1,0:T(8,128)(2,1)} async-done(((bf16[24,53,2048]{2,1,0:T(8,128)(2,1)}), bf16[24,53,2048]{2,1,0:T(8,128)(2,1)}, u32[]{:S(2)}, u32[]{:S(2)}) %all-to-all-start) | async-done | bytes 5210144 | tf_op jit(solution)/shard_map/all_to_all | solution.py:158
  944.8 5.9 copy.179
  950.7 6.5 all_to_all.51
  957.2 63.6 %all-gather.15.cloned.1.call-done = bf16[2048,3,2048]{2,0,1:T(8,128)(2,1)} async-done(((bf16[512,3,2048]{2,0,1:T(8,128)(2,1)}), bf16[2048,3,2048]{2,0,1:T(8,128)(2,1)}) %all-gather.15.cloned.1.call-update) | async-done | bytes 25165840 | tf_op jit(solution)/shard_map/all_gather | solution.py:173
  1020.8 11.6 fusion.2
  1032.4 15.5 multiply_convert_fusion.1
  1047.9 12.0 convolution_convert_fusion.1
  1059.9 9.8 copy.180
  1069.7 5.5 all-to-all-start.1
  1075.2 11.8 fusion
  1087.0 15.7 add_convert_fusion
  1102.7 9.9 copy.185
  1112.5 115.3 %all-to-all-done.1 = bf16[3,424,2048]{2,0,1:T(4,128)(2,1)} async-done(((bf16[3,424,2048]{2,0,1:T(4,128)(2,1)}), bf16[3,424,2048]{2,0,1:T(4,128)(2,1)}, u32[]{:S(2)}, u32[]{:S(2)}) %all-to-all-start.1) | async-done | bytes 5210144 | tf_op jit(solution)/shard_map/all_to_all | solution.py:216
  1227.9 4.9 all-to-all-start.3
  1233.3 9.3 copy.253
  1242.6 6.6 reshape.417
  1249.2 135.3 %all-to-all-done.3 = bf16[3,424,2048]{2,0,1:T(4,128)(2,1)} async-done(((bf16[3,424,2048]{2,0,1:T(4,128)(2,1)}), bf16[3,424,2048]{2,0,1:T(4,128)(2,1)}, u32[]{:S(2)}, u32[]{:S(2)}) %all-to-all-start.3) | async-done | bytes 5210144 | tf_op jit(solution)/shard_map/all_to_all | solution.py:217
  1384.5 9.3 copy.252
  1393.8 6.5 reshape.419
  1400.3 12.0 gather_fusion
  1412.3 12.1 gather_fusion.1
  1424.5 5.2 convert_reduce_fusion
  1430.1 6.7 fusion.8
  1444.2 5.6 multiply_convert_fusion.4
  1453.4 4.0 copy.222
  1457.5 5.0 convolution_convert_fusion.3
  1462.4 4.1 copy.201
  1466.6 5.7 convert_bitcast_fusion.3
  1473.1 14.0 reduce-scatter.19.cloned.1.call-done
  1502.5 19.3 reduce-scatter.13.cloned.1.call-done
  1521.8 12.8 convolution_convert_fusion
  1534.7 22.9 pad_maximum_fusion.1
  1557.6 12.4 convert_bitcast_fusion
  1570.0 12.3 convert_bitcast_fusion.2
  1582.3 9.7 convert_bitcast_fusion.1
  1592.9 14.8 fusion.33
  1609.2 27.5 %pad_maximum_fusion = bf16[2048,3,3072]{0,2,1:T(8,128)(2,1)} fusion(bf16[2048,3,1024]{0,2,1:T(8,128)(2,1)} %convert_bitcast_fusion, bf16[2048,3,1024]{0,2,1:T(8,128)(2,1)} %convert_bitcast_fusion.1, bf16[2048,3,1024]{0,2,1:T(8,128)(2,1)} %convert_bitcast_fusion.2), kind=kLoop, calls=%fused_computation.5 | loop fusion | flops 113246208 | bytes 75497472 | tf_op jit(solution)/shard_map/concatenate | solution.py:203
  1636.8 463.8 %reduce-scatter.15.cloned.1.call-done = bf16[256,4,2048]{2,0,1:T(8,128)(2,1)} async-done(((bf16[2048,4,2048]{2,0,1:T(8,128)(2,1)}), bf16[256,4,2048]{2,0,1:T(8,128)(2,1)}) %reduce-scatter.15.cloned.1.call-update) | async-done | bytes 4194320 | tf_op jit(solution)/shard_map/reduce_scatter | solution.py:286
  2101.9 62.9 %reduce-scatter.23.cloned.1.call-done = f32[16,2]{1,0:T(8,128)} async-done(((f32[128,2]{1,0:T(8,128)}), f32[16,2]{1,0:T(8,128)}) %reduce-scatter.23.cloned.1.call-update) | async-done | bytes 144
  2165.6 65.7 %reduce-scatter.21.cloned.1.call-done = f32[256,2]{1,0:T(8,128)} async-done(((f32[2048,2]{1,0:T(8,128)}), f32[256,2]{1,0:T(8,128)}) %reduce-scatter.21.cloned.1.call-update) | async-done | bytes 2064
  2232.3 5.7 all-reduce.4
  2239.1 255.4 %reduce-scatter.17.cloned.1.call-done = bf16[512,3,3072]{0,2,1:T(8,128)(2,1)} async-done(((bf16[2048,3,3072]{0,2,1:T(8,128)(2,1)}), bf16[512,3,3072]{0,2,1:T(8,128)(2,1)}) %reduce-scatter.17.cloned.1.call-update) | async-done | bytes 9437200 | tf_op jit(solution)/shard_map/reduce_scatter | solution.py:202
  2494.5 5.5 slice.119
  2500.0 6.6 copy.206
  2506.6 9.2 slice.118
  2515.8 12.8 copy.205
  2528.6 53.8 %all-reduce.7.cloned.1.call-done = bf16[256,4,2048]{2,0,1:T(8,128)(2,1)} async-done(((bf16[256,4,2048]{2,0,1:T(8,128)(2,1)}), bf16[256,4,2048]{2,0,1:T(8,128)(2,1)}) %all-reduce.7.cloned.1.call-update) | async-done | bytes 4194320 | tf_op jit(solution)/shard_map/psum | solution.py:299
  (272 shorter events, 72.0 us)
Async XLA Ops:
  7.2 485.6 %all-gather.9.cloned.1.call-start = ((), (), s32[]{:S(2)}) async-start(), calls=%async_computation.10 | async-start | bytes 28311552 | tf_op jit(solution)/shard_map/all_gather | solution.py:68
  7.9 555.2 %all-gather.19.cloned.1.call-start = ((), (), s32[]{:S(2)}) async-start(), calls=%async_computation.19 | async-start | bytes 2621440 | tf_op jit(solution)/shard_map/all_gather | solution.py:92
  60.5 442.6 %copy-start.47 = (f32[128]{0:T(128)}, f32[128]{0:T(128)S(1)}, u32[]{:S(2)}) copy-start(f32[128]{0:T(128)S(1)} %fusion.58) | copy-start | bytes 1540
  60.5 442.6 %copy-start.31 = (f32[2048,1]{0,1:T(1,128)}, f32[2048,1]{0,1:T(1,128)S(1)}, u32[]{:S(2)}) copy-start(f32[2048,1]{0,1:T(1,128)S(1)} %get-tuple-element.161) | copy-start | bytes 24580
  60.5 726.4 %copy-start.33 = (f32[2048,1]{0,1:T(1,128)}, f32[2048,1]{0,1:T(1,128)S(1)}, u32[]{:S(2)}) copy-start(f32[2048,1]{0,1:T(1,128)S(1)} %get-tuple-element.160) | copy-start | bytes 24580
  492.8 11.2 copy-start.53
  492.8 11.7 copy-start.60
  504.0 63.0 %all-gather.11.cloned.1.call-start = ((), (), s32[]{:S(2)}) async-start(), calls=%async_computation.11 | async-start | bytes 2621440 | tf_op jit(solution)/shard_map/all_gather | solution.py:91
  524.0 4.4 copy-start.51
  524.4 4.5 copy-start.26
  524.4 4.5 copy-start.28
  529.6 37.3 %copy-start.15 = (bf16[128,16,64]{2,0,1:T(8,128)(2,1)}, bf16[128,16,64]{2,0,1:T(8,128)(2,1)S(1)}, u32[]{:S(2)}) copy-start(bf16[128,16,64]{2,0,1:T(8,128)(2,1)S(1)} %get-tuple-element.148) | copy-start | bytes 786436
  529.7 37.3 %copy-start.17 = (bf16[128,16,64]{2,0,1:T(8,128)(2,1)}, bf16[128,16,64]{2,0,1:T(8,128)(2,1)S(1)}, u32[]{:S(2)}) copy-start(bf16[128,16,64]{2,0,1:T(8,128)(2,1)S(1)} %get-tuple-element.149) | copy-start | bytes 786436
  531.0 251.0 %all-gather.13.cloned.1.call-start = ((), (), s32[]{:S(2)}) async-start(), calls=%async_computation.12 | async-start | bytes 9437184 | tf_op jit(solution)/shard_map/all_gather | solution.py:69
  531.6 9.2 copy-start.19
  531.6 332.9 %all-gather.17.cloned.1.call-start = ((), (), s32[]{:S(2)}) async-start(), calls=%async_computation.14 | async-start | bytes 15728640 | tf_op jit(solution)/shard_map/all_gather | solution.py:183
  532.2 488.6 %all-gather.15.cloned.1.call-start = ((), (), s32[]{:S(2)}) async-start(), calls=%async_computation.13 | async-start | bytes 31457280 | tf_op jit(solution)/shard_map/all_gather | solution.py:173
  557.6 260.7 %all-to-all-start.2 = ((bf16[24,53,2048]{2,1,0:T(8,128)(2,1)}), bf16[24,53,2048]{2,1,0:T(8,128)(2,1)}, u32[]{:S(2)}, u32[]{:S(2)}) async-start(bf16[24,53,2048]{2,1,0:T(8,128)(2,1)} %reshape.418), calls=%async_computation.2 | async-start | bytes 11010048 | tf_op jit(solution)/shard_map/all_to_all | solution.py:165
  563.1 8.1 copy-start.23
  566.9 4.9 copy-start.21
  571.1 210.9 %copy-start.8 = (bf16[1,128,2048]{2,1,0:T(8,128)(2,1)S(1)}, bf16[1,128,2048]{2,1,0:T(8,128)(2,1)}, u32[]{:S(2)}) copy-start(bf16[1,128,2048]{2,1,0:T(8,128)(2,1)} %param.11) | copy-start | bytes 1572868
  571.2 215.6 %copy-start.43 = (f32[16,128]{1,0:T(8,128)}, f32[16,128]{1,0:T(8,128)S(1)}, u32[]{:S(2)}) copy-start(f32[16,128]{1,0:T(8,128)S(1)} %log_add_fusion) | copy-start | bytes 24580
  575.0 211.8 %copy-start.13 = (bf16[128,16,128]{0,2,1:T(8,128)(2,1)}, bf16[128,16,128]{0,2,1:T(8,128)(2,1)S(1)}, u32[]{:S(2)}) copy-start(bf16[128,16,128]{0,2,1:T(8,128)(2,1)S(1)} %get-tuple-element.168) | copy-start | bytes 1572868
  786.8 31.4 %copy-start.56 = (f32[128]{0:T(128)}, f32[128]{0:T(128)S(1)}, u32[]{:S(2)}) copy-start(f32[128]{0:T(128)S(1)} %get-tuple-element.170) | copy-start | bytes 1540
  786.8 31.4 %copy-start.54 = (f32[128]{0:T(128)}, f32[128]{0:T(128)S(1)}, u32[]{:S(2)}) copy-start(f32[128]{0:T(128)S(1)} %fusion.59) | copy-start | bytes 1540
  818.3 126.5 %all-to-all-start = ((bf16[24,53,2048]{2,1,0:T(8,128)(2,1)}), bf16[24,53,2048]{2,1,0:T(8,128)(2,1)}, u32[]{:S(2)}, u32[]{:S(2)}) async-start(bf16[24,53,2048]{2,1,0:T(8,128)(2,1)} %reshape.416), calls=%async_computation | async-start | bytes 11010048 | tf_op jit(solution)/shard_map/all_to_all | solution.py:158
  1047.9 39.0 %copy-start.61 = (bf16[3,424,1024]{2,1,0:T(8,128)(2,1)}, bf16[3,424,1024]{2,1,0:T(8,128)(2,1)S(1)}, u32[]{:S(2)}) copy-start(bf16[3,424,1024]{2,1,0:T(8,128)(2,1)S(1)} %get-tuple-element.139) | copy-start | bytes 7815172
  1069.7 158.2 %all-to-all-start.1 = ((bf16[3,424,2048]{2,0,1:T(4,128)(2,1)}), bf16[3,424,2048]{2,0,1:T(4,128)(2,1)}, u32[]{:S(2)}, u32[]{:S(2)}) async-start(bf16[3,424,2048]{2,0,1:T(4,128)(2,1)} %copy.180), calls=%async_computation.1 | async-start | bytes 13893632 | tf_op jit(solution)/shard_map/all_to_all | solution.py:216
  1227.9 156.7 %all-to-all-start.3 = ((bf16[3,424,2048]{2,0,1:T(4,128)(2,1)}), bf16[3,424,2048]{2,0,1:T(4,128)(2,1)}, u32[]{:S(2)}, u32[]{:S(2)}) async-start(bf16[3,424,2048]{2,0,1:T(4,128)(2,1)} %copy.185), calls=%async_computation.3 | async-start | bytes 13893632 | tf_op jit(solution)/shard_map/all_to_all | solution.py:217
  1232.8 254.3 %reduce-scatter.19.cloned.1.call-start = ((), (), s32[]{:S(2)}) async-start(), calls=%async_computation.20 | async-start | bytes 2621440
  1412.3 17.4 copy-start.34
  1412.3 17.4 copy-start.55
  1424.4 5.3 copy-start.7
  1424.5 5.6 copy-start.57
  1424.5 12.3 copy-start.20
  1424.5 13.5 slice-start
  1430.1 7.9 slice-start.1
  1444.1 6.9 copy-start.16
  1444.1 6.9 copy-start.18
  1451.1 6.4 copy-start.22
  1457.4 9.2 copy-start.14
  1457.4 64.4 %reduce-scatter.13.cloned.1.call-start = ((), (), s32[]{:S(2)}) async-start(), calls=%async_computation.15 | async-start | bytes 2621440 | tf_op jit(solution)/shard_map/reduce_scatter | solution.py:270
  1466.5 634.1 %reduce-scatter.15.cloned.1.call-start = ((), (), s32[]{:S(2)}) async-start(), calls=%async_computation.16 | async-start | bytes 37748736 | tf_op jit(solution)/shard_map/reduce_scatter | solution.py:286
  1466.6 5.7 copy-start.10
  1466.6 5.7 copy-start.12
  1472.3 20.7 copy-start.27
  1472.3 20.7 copy-start.29
  1490.6 4.9 copy-start.3
  1490.6 4.9 copy-start.36
  1490.6 4.9 copy-start.50
  1497.4 24.4 copy-start.9
  1497.4 24.4 copy-start.32
  1497.4 24.4 copy-start.48
  1557.5 607.3 %reduce-scatter.23.cloned.1.call-start = ((), (), s32[]{:S(2)}) async-start(), calls=%async_computation.22 | async-start | bytes 73728
  1557.6 12.4 copy-start.62
  1557.6 24.7 slice-start.2
  1570.0 12.3 slice-start.3
  1570.0 12.3 copy-start.63
  1582.3 10.6 copy-start.30
  1592.8 638.5 %reduce-scatter.21.cloned.1.call-start = ((), (), s32[]{:S(2)}) async-start(), calls=%async_computation.21 | async-start | bytes 1179648
  1609.1 885.4 %reduce-scatter.17.cloned.1.call-start = ((), (), s32[]{:S(2)}) async-start(), calls=%async_computation.18 | async-start | bytes 47185920 | tf_op jit(solution)/shard_map/reduce_scatter | solution.py:202
  1636.7 463.9 %copy-start.59 = (f32[128]{0:T(128)S(1)}, f32[128]{0:T(128)}, u32[]{:S(2)}) copy-start(f32[128]{0:T(128)} %copy-done.58) | copy-start | bytes 1540
  1636.7 464.0 %copy-start.25 = (f32[128,2048]{1,0:T(8,128)S(1)}, f32[128,2048]{1,0:T(8,128)}, u32[]{:S(2)}) copy-start(f32[128,2048]{1,0:T(8,128)} %get-tuple-element.172) | copy-start | bytes 3145732
  1636.8 945.7 %all-reduce.7.cloned.1.call-start = ((), (), s32[]{:S(2)}) async-start(), calls=%async_computation.17 | async-start | bytes 8388608 | tf_op jit(solution)/shard_map/psum | solution.py:299
  (21 other events, 47.6 us)
Sparse Core Ops, SparseCore 0:
  9.5 483.2 all-gather.8
  504.1 22.5 all-gather.18
  531.1 20.5 all-gather.10
  553.7 228.2 all-gather.12
  783.4 81.0 all-gather.16
  866.0 154.8 all-gather.14
  1457.5 29.5 reduce-scatter.18
  1490.3 31.4 reduce-scatter.12
  1557.7 542.9 reduce-scatter.14
  2104.4 60.3 reduce-scatter.22
  2168.8 62.4 reduce-scatter.20
  2234.0 260.5 reduce-scatter.16
  2496.9 85.5 all-reduce.6
where the time goes:
time: 2610 us; the launch traced here: 2600 us
  waiting for transfers between devices  1990 us (76%)
  local copies, waits for them, and re-layouts  213 us (8%)
  matrix products  184 us (7%)
  other arithmetic  102 us (4%)
  blocking collectives  75.5 us (3%)
    reduce_scatter x1, waiting for transfers between devices, body(): lax.psum_scatter(jnp.concatenate([projections, output_part[:, None, :]],...  464 us
    all_gather x1, waiting for transfers between devices, body(): lax.all_gather(qkv_w, 'fsdp', axis=0, tiled=True)  432 us
    reduce_scatter x1, waiting for transfers between devices, body(): lax.psum_scatter(jnp.concatenate([jnp.einsum('erd,erk->dek', got_rows, ga...  255 us
    all_gather x1, waiting for transfers between devices, body(): lax.all_gather(out_w, 'fsdp', axis=0, tiled=True)  207 us
    unnamed x16, waiting for transfers between devices  145 us
    all_to_all x1, waiting for transfers between devices, body(): lax.all_to_all(input_grads, 'fsdp', split_axis=1, concat_axis=0, tiled=True)  135 us
    all_to_all x1, waiting for transfers between devices, body(): lax.all_to_all(made_rows, 'fsdp', split_axis=1, concat_axis=0, tiled=True)  115 us
    all_to_all x1, waiting for transfers between devices, body(): lax.all_to_all(send_rows.reshape(experts_all, capacity, model_width), 'fs...  68.4 us
  transfers between devices with their start and end apart: 17, of which 14 were waited for; matrix products, arithmetic and copies ran while one was open for 12% of the time, Pallas kernels for 0%

commit v1 on v0

--- a/solution.py
+++ b/solution.py
@@ -7,6 +7,14 @@
 EPS = 1e-06
 ROPE_BASE = 10000.0
 NEG_FILL = -1e30
+
+
+def _track_pipes(obj):
+    items = [obj]
+    q_n = lax.axis_size("ctx")
+    for k0 in range(q_n - 1):
+        items.append(lax.ppermute(items[-1], "ctx", [(nth, (nth + 1) % q_n) for nth in range(q_n)]))
+    return jnp.roll(jnp.concatenate(items[::-1], 0), (lax.axis_index("ctx") + 1) * obj.shape[0], 0)
 
 
 def rms_scale(values, gain):
@@ -170,7 +178,7 @@
             tiled=True,
         ),
     )
-    segment = lax.all_gather(gate_up, "ctx", axis=0, tiled=True)
+    segment = _track_pipes(gate_up)
     gate_add = jnp.einsum(
         "erd,dek->erk", got_rows, segment[:, :, :hidden_units], preferred_element_type=f32
     )

time: 2610 us -> 2560 us (0.981)
  waiting for transfers between devices: 1990 us -> 1880 us
  local copies, waits for them, and re-layouts: 213 us -> 264 us
    all_gather x1, waiting for transfers between devices: 207 us -> 29.9 us  [body(): lax.all_gather(out_w, 'fsdp', axis=0, tiled=True)]
    ppermute x0 -> x3, waiting for transfers between devices: none -> 122 us  [_track_pipes(): lax.ppermute(items[-1], 'ctx', [(nth, (nth + 1) % q_n) for nth in range(q...]
    unnamed x155 -> x164, local copies, waits for them, and re-layouts: 44.9 us -> 92.9 us
    all_to_all x1, waiting for transfers between devices: 0.01 us -> 35.5 us  [body(): lax.all_to_all(send_grads.reshape(experts_all, capacity, model_width), 'f...]
    all_gather x1, waiting for transfers between devices: 63.6 us -> 28.9 us  [body(): segment = lax.all_gather(gate_up, 'ctx', axis=0, tiled=True)]
    all_gather x1, waiting for transfers between devices: 29.1 us -> 0.01 us  [body(): segment = lax.all_gather(down_t, 'ctx', axis=0, tiled=True)]
  transfers between devices with their start and end apart: 17 -> 20, of which waited for: 14 -> 16; matrix products, arithmetic and copies ran while one was open for 12% -> 15% of each run, Pallas kernels for 0% -> 0%
where the time goes in v1:
time: 2560 us; the launch traced here: 2550 us
  waiting for transfers between devices  1880 us (73%)
  local copies, waits for them, and re-layouts  264 us (10%)
  matrix products  188 us (7%)
  other arithmetic  101 us (4%)
  blocking collectives  75.5 us (3%)
    reduce_scatter x1, waiting for transfers between devices, body(): lax.psum_scatter(jnp.concatenate([projections, output_part[:, None, :]],...  465 us
    all_gather x1, waiting for transfers between devices, body(): lax.all_gather(qkv_w, 'fsdp', axis=0, tiled=True)  432 us
    reduce_scatter x1, waiting for transfers between devices, body(): lax.psum_scatter(jnp.concatenate([jnp.einsum('erd,erk->dek', got_rows, ga...  255 us
    unnamed x16, waiting for transfers between devices  144 us
    all_to_all x1, waiting for transfers between devices, body(): lax.all_to_all(input_grads, 'fsdp', split_axis=1, concat_axis=0, tiled=True)  129 us
    ppermute x3, waiting for transfers between devices, _track_pipes(): lax.ppermute(items[-1], 'ctx', [(nth, (nth + 1) % q_n) for nth in range(q...  122 us
    all_to_all x1, waiting for transfers between devices, body(): lax.all_to_all(made_rows, 'fsdp', split_axis=1, concat_axis=0, tiled=True)  118 us
    unnamed x164, local copies, waits for them, and re-layouts  92.9 us
  transfers between devices with their start and end apart: 20, of which 16 were waited for; matrix products, arithmetic and copies ran while one was open for 15% of the time, Pallas kernels for 0%

profile of v1, /device:TPU:0, one launch (start us, length us, event | category | flops | bytes accessed | tf_op | source)
XLA Modules:
  0.0 2548.2 jit_solution(13914272970009343476)
XLA Ops:
  7.9 50.7 %all_gather.24 = bf16[2048,2]{0,1:T(2,128)(2,1)S(1)} all-gather(bf16[256,2]{0,1:T(2,128)(2,1)} %param.17), channel_id=1, replica_groups=mesh['ctx'=4,'fsdp'=8] {'fsdp'}, dimensions={0}, use_global_device_ids=true | all-gather | bytes 9216 | tf_op jit(solution)/shard_map/all_gather | solution.py:78
  60.4 432.4 %all-gather.9.cloned.1.call-done = bf16[2048,3,2048]{2,0,1:T(8,128)(2,1)} async-done(((bf16[256,3,2048]{2,0,1:T(8,128)(2,1)}), bf16[2048,3,2048]{2,0,1:T(8,128)(2,1)}) %all-gather.9.cloned.1.call-update) | async-done | bytes 25165840 | tf_op jit(solution)/shard_map/all_gather | solution.py:76
  492.8 10.3 fusion.52
  504.1 19.2 all-gather.1
  533.2 6.8 reduce-window.36
  541.0 73.9 %collective-permute-done = bf16[512,3,2048]{2,0,1:T(8,128)(2,1)} collective-permute-done((bf16[512,3,2048]{2,0,1:T(8,128)(2,1)}, bf16[512,3,2048]{2,0,1:T(8,128)(2,1)}, u32[]{:S(2)}, u32[]{:S(2)}) %collective-permute-start) | collective-permute-done | bytes 6291488 | tf_op jit(solution)/shard_map/ppermute | solution.py:16
  615.3 10.1 scatter_custom_fusion.1
  625.4 6.5 reshape.418
  637.4 48.6 %collective-permute-done.1 = bf16[512,3,2048]{2,0,1:T(8,128)(2,1)} collective-permute-done((bf16[512,3,2048]{2,0,1:T(8,128)(2,1)}, bf16[512,3,2048]{2,0,1:T(8,128)(2,1)}, u32[]{:S(2)}, u32[]{:S(2)}) %collective-permute-start.1) | collective-permute-done | bytes 6291488 | tf_op jit(solution)/shard_map/ppermute | solution.py:16
  697.6 29.9 %all-gather.13.cloned.1.call-done = bf16[2048,2048]{1,0:T(8,128)(2,1)} async-done(((bf16[256,2048]{1,0:T(8,128)(2,1)}), bf16[2048,2048]{1,0:T(8,128)(2,1)}) %all-gather.13.cloned.1.call-update) | async-done | bytes 8388624 | tf_op jit(solution)/shard_map/all_gather | solution.py:77
  733.4 23.3 scatter_custom_fusion
  756.7 6.9 reshape.416
  763.6 35.5 %all-to-all-done.2 = bf16[24,53,2048]{2,1,0:T(8,128)(2,1)} async-done(((bf16[24,53,2048]{2,1,0:T(8,128)(2,1)}), bf16[24,53,2048]{2,1,0:T(8,128)(2,1)}, u32[]{:S(2)}, u32[]{:S(2)}) %all-to-all-start.2) | async-done | bytes 5210144 | tf_op jit(solution)/shard_map/all_to_all | solution.py:173
  803.8 5.9 copy.184
  809.7 6.5 all_to_all.58
  816.2 6.5 constant_dynamic-update-slice_fusion.7
  822.8 6.8 constant_dynamic-update-slice_fusion.6
  829.6 6.7 constant_dynamic-update-slice_fusion.5
  839.5 6.9 constant_dynamic-update-slice_fusion.3
  846.4 8.7 constant_dynamic-update-slice_fusion.2
  855.1 8.5 constant_dynamic-update-slice_fusion.1
  866.8 11.5 fusion.71
  878.3 47.3 %all-to-all-done = bf16[24,53,2048]{2,1,0:T(8,128)(2,1)} async-done(((bf16[24,53,2048]{2,1,0:T(8,128)(2,1)}), bf16[24,53,2048]{2,1,0:T(8,128)(2,1)}, u32[]{:S(2)}, u32[]{:S(2)}) %all-to-all-start) | async-done | bytes 5210144 | tf_op jit(solution)/shard_map/all_to_all | solution.py:166
  925.6 6.0 copy.179
  931.6 6.5 all_to_all.51
  938.1 11.6 fusion.4
  949.7 15.7 multiply_convert_fusion.1
  965.4 28.9 %all-gather.17.cloned.1.call-done = bf16[2048,3,2048]{2,0,1:T(8,128)(2,1)} async-done(((bf16[512,3,2048]{2,0,1:T(8,128)(2,1)}), bf16[2048,3,2048]{2,0,1:T(8,128)(2,1)}) %all-gather.17.cloned.1.call-update) | async-done | bytes 25165840 | tf_op jit(solution)/shard_map/all_gather | solution.py:202
  994.3 11.8 fusion
  1006.0 15.7 add_convert_fusion
  1021.8 9.9 copy.185
  1031.6 6.2 all-to-all-start.3
  1037.9 14.0 convolution_convert_fusion.1
  1051.9 9.9 copy.180
  1061.7 128.8 %all-to-all-done.3 = bf16[3,424,2048]{2,0,1:T(4,128)(2,1)} async-done(((bf16[3,424,2048]{2,0,1:T(4,128)(2,1)}), bf16[3,424,2048]{2,0,1:T(4,128)(2,1)}, u32[]{:S(2)}, u32[]{:S(2)}) %all-to-all-start.3) | async-done | bytes 5210144 | tf_op jit(solution)/shard_map/all_to_all | solution.py:225
  1195.5 9.3 copy.252
  1204.8 6.7 reshape.419
  1211.4 12.0 gather_fusion.1
  1228.9 118.2 %all-to-all-done.1 = bf16[3,424,2048]{2,0,1:T(4,128)(2,1)} async-done(((bf16[3,424,2048]{2,0,1:T(4,128)(2,1)}), bf16[3,424,2048]{2,0,1:T(4,128)(2,1)}, u32[]{:S(2)}, u32[]{:S(2)}) %all-to-all-start.1) | async-done | bytes 5210144 | tf_op jit(solution)/shard_map/all_to_all | solution.py:224
  1347.1 9.3 copy.253
  1356.4 6.5 reshape.417
  1362.9 12.1 gather_fusion
  1375.0 6.6 fusion.8
  1382.8 6.3 fusion.31
  1416.0 5.7 convert_bitcast_fusion.3
  1422.5 13.6 reduce-scatter.19.cloned.1.call-done
  1451.4 19.4 reduce-scatter.13.cloned.1.call-done
  1470.8 12.9 convolution_convert_fusion
  1483.6 22.9 pad_maximum_fusion.1
  1506.8 12.4 convert_bitcast_fusion.1
  1519.2 12.3 convert_bitcast_fusion.2
  1531.5 9.8 convert_bitcast_fusion
  1542.4 14.7 fusion.33
  1558.5 26.5 %pad_maximum_fusion = bf16[2048,3,3072]{0,2,1:T(8,128)(2,1)} fusion(bf16[2048,3,1024]{0,2,1:T(8,128)(2,1)} %convert_bitcast_fusion, bf16[2048,3,1024]{0,2,1:T(8,128)(2,1)} %convert_bitcast_fusion.1, bf16[2048,3,1024]{0,2,1:T(8,128)(2,1)} %convert_bitcast_fusion.2), kind=kLoop, calls=%fused_computation.5 | loop fusion | flops 113246208 | bytes 75497472 | tf_op jit(solution)/shard_map/concatenate | solution.py:211
  1585.1 465.0 %reduce-scatter.15.cloned.1.call-done = bf16[256,4,2048]{2,0,1:T(8,128)(2,1)} async-done(((bf16[2048,4,2048]{2,0,1:T(8,128)(2,1)}), bf16[256,4,2048]{2,0,1:T(8,128)(2,1)}) %reduce-scatter.15.cloned.1.call-update) | async-done | bytes 4194320 | tf_op jit(solution)/shard_map/reduce_scatter | solution.py:294
  2051.4 62.8 %reduce-scatter.23.cloned.1.call-done = f32[16,2]{1,0:T(8,128)} async-done(((f32[128,2]{1,0:T(8,128)}), f32[16,2]{1,0:T(8,128)}) %reduce-scatter.23.cloned.1.call-update) | async-done | bytes 144
  2115.0 65.6 %reduce-scatter.21.cloned.1.call-done = f32[256,2]{1,0:T(8,128)} async-done(((f32[2048,2]{1,0:T(8,128)}), f32[256,2]{1,0:T(8,128)}) %reduce-scatter.21.cloned.1.call-update) | async-done | bytes 2064
  2181.6 5.7 all-reduce.4
  2188.4 255.4 %reduce-scatter.17.cloned.1.call-done = bf16[512,3,3072]{0,2,1:T(8,128)(2,1)} async-done(((bf16[2048,3,3072]{0,2,1:T(8,128)(2,1)}), bf16[512,3,3072]{0,2,1:T(8,128)(2,1)}) %reduce-scatter.17.cloned.1.call-update) | async-done | bytes 9437200 | tf_op jit(solution)/shard_map/reduce_scatter | solution.py:210
  2443.8 9.5 slice.124
  2453.3 12.8 copy.205
  2466.1 5.5 slice.125
  2471.7 6.6 copy.206
  2478.3 53.4 %all-reduce.7.cloned.1.call-done = bf16[256,4,2048]{2,0,1:T(8,128)(2,1)} async-done(((bf16[256,4,2048]{2,0,1:T(8,128)(2,1)}), bf16[256,4,2048]{2,0,1:T(8,128)(2,1)}) %all-reduce.7.cloned.1.call-update) | async-done | bytes 4194320 | tf_op jit(solution)/shard_map/psum | solution.py:307
  (288 shorter events, 119.4 us)
Async XLA Ops:
  7.2 485.6 %all-gather.9.cloned.1.call-start = ((), (), s32[]{:S(2)}) async-start(), calls=%async_computation.10 | async-start | bytes 28311552 | tf_op jit(solution)/shard_map/all_gather | solution.py:76
  7.9 678.1 %all-gather.19.cloned.1.call-start = ((), (), s32[]{:S(2)}) async-start(), calls=%async_computation.19 | async-start | bytes 2621440 | tf_op jit(solution)/shard_map/all_gather | solution.py:100
  60.4 442.7 %copy-start.47 = (f32[128]{0:T(128)}, f32[128]{0:T(128)S(1)}, u32[]{:S(2)}) copy-start(f32[128]{0:T(128)S(1)} %fusion.60) | copy-start | bytes 1540
  60.4 442.7 %copy-start.30 = (f32[2048,1]{0,1:T(1,128)}, f32[2048,1]{0,1:T(1,128)S(1)}, u32[]{:S(2)}) copy-start(f32[2048,1]{0,1:T(1,128)S(1)} %get-tuple-element.161) | copy-start | bytes 24580
  60.4 671.9 %copy-start.32 = (f32[2048,1]{0,1:T(1,128)}, f32[2048,1]{0,1:T(1,128)S(1)}, u32[]{:S(2)}) copy-start(f32[2048,1]{0,1:T(1,128)S(1)} %get-tuple-element.160) | copy-start | bytes 24580
  492.8 11.3 copy-start.53
  492.8 11.3 copy-start.60
  504.0 185.5 %all-gather.11.cloned.1.call-start = ((), (), s32[]{:S(2)}) async-start(), calls=%async_computation.11 | async-start | bytes 2621440 | tf_op jit(solution)/shard_map/all_gather | solution.py:99
  529.7 159.9 %copy-start.15 = (bf16[128,16,64]{2,0,1:T(8,128)(2,1)}, bf16[128,16,64]{2,0,1:T(8,128)(2,1)S(1)}, u32[]{:S(2)}) copy-start(bf16[128,16,64]{2,0,1:T(8,128)(2,1)S(1)} %get-tuple-element.148) | copy-start | bytes 786436
  529.7 159.8 %copy-start.17 = (bf16[128,16,64]{2,0,1:T(8,128)(2,1)}, bf16[128,16,64]{2,0,1:T(8,128)(2,1)S(1)}, u32[]{:S(2)}) copy-start(bf16[128,16,64]{2,0,1:T(8,128)(2,1)S(1)} %get-tuple-element.149) | copy-start | bytes 786436
  531.1 196.4 %all-gather.13.cloned.1.call-start = ((), (), s32[]{:S(2)}) async-start(), calls=%async_computation.12 | async-start | bytes 9437184 | tf_op jit(solution)/shard_map/all_gather | solution.py:77
  531.6 8.9 copy-start.44
  531.7 9.2 copy-start.19
  531.7 335.1 %all-gather.15.cloned.1.call-start = ((), (), s32[]{:S(2)}) async-start(), calls=%async_computation.13 | async-start | bytes 15728640 | tf_op jit(solution)/shard_map/all_gather | solution.py:191
  532.3 462.0 %all-gather.17.cloned.1.call-start = ((), (), s32[]{:S(2)}) async-start(), calls=%async_computation.14 | async-start | bytes 31457280 | tf_op jit(solution)/shard_map/all_gather | solution.py:202
  532.8 82.0 %collective-permute-start = (bf16[512,3,2048]{2,0,1:T(8,128)(2,1)}, bf16[512,3,2048]{2,0,1:T(8,128)(2,1)}, u32[]{:S(2)}, u32[]{:S(2)}) collective-permute-start(bf16[512,3,2048]{2,0,1:T(8,128)(2,1)} %param.19), channel_id=1, source_target_pairs={{0,8},{8,16},{16,24},{24,0},{1,9},{9,17},{17,25},{25,1},{2,10},{10... | collective-permute-start | bytes 18874376 | tf_op jit(solution)/shard_map/ppermute | solution.py:16
  614.8 71.2 %collective-permute-start.1 = (bf16[512,3,2048]{2,0,1:T(8,128)(2,1)}, bf16[512,3,2048]{2,0,1:T(8,128)(2,1)}, u32[]{:S(2)}, u32[]{:S(2)}) collective-permute-start(bf16[512,3,2048]{2,0,1:T(8,128)(2,1)} %collective-permute-done), channel_id=1, source_target_pairs={{0,8},{8,16},{16,24},{24,0},{1,9},{9,17},{17,25},{25,1},{2,10},{10... | collective-permute-start | bytes 18874376 | tf_op jit(solution)/shard_map/ppermute | solution.py:16
  631.9 167.2 %all-to-all-start.2 = ((bf16[24,53,2048]{2,1,0:T(8,128)(2,1)}), bf16[24,53,2048]{2,1,0:T(8,128)(2,1)}, u32[]{:S(2)}, u32[]{:S(2)}) async-start(bf16[24,53,2048]{2,1,0:T(8,128)(2,1)} %reshape.418), calls=%async_computation.2 | async-start | bytes 11010048 | tf_op jit(solution)/shard_map/all_to_all | solution.py:173
  637.4 56.4 %copy-start.22 = (pred[128,512]{1,0:T(8,128)(4,1)}, pred[128,512]{1,0:T(8,128)(4,1)S(1)}, u32[]{:S(2)}) copy-start(pred[128,512]{1,0:T(8,128)(4,1)S(1)} %broadcast_compare_fusion) | copy-start | bytes 196612
  686.0 130.2 %collective-permute-start.2 = (bf16[512,3,2048]{2,0,1:T(8,128)(2,1)}, bf16[512,3,2048]{2,0,1:T(8,128)(2,1)}, u32[]{:S(2)}, u32[]{:S(2)}) collective-permute-start(bf16[512,3,2048]{2,0,1:T(8,128)(2,1)} %collective-permute-done.1), channel_id=1, source_target_pairs={{0,8},{8,16},{16,24},{24,0},{1,9},{9,17},{17,25},{25,1},{2,10},{10... | collective-permute-start | bytes 18874376 | tf_op jit(solution)/shard_map/ppermute | solution.py:16
  693.7 33.7 %copy-start.8 = (bf16[1,128,2048]{2,1,0:T(8,128)(2,1)S(1)}, bf16[1,128,2048]{2,1,0:T(8,128)(2,1)}, u32[]{:S(2)}) copy-start(bf16[1,128,2048]{2,1,0:T(8,128)(2,1)} %param.11) | copy-start | bytes 1572868
  693.8 38.4 %copy-start.42 = (f32[16,128]{1,0:T(8,128)}, f32[16,128]{1,0:T(8,128)S(1)}, u32[]{:S(2)}) copy-start(f32[16,128]{1,0:T(8,128)S(1)} %log_add_fusion) | copy-start | bytes 24580
  697.6 34.6 %copy-start.13 = (bf16[128,16,128]{0,2,1:T(8,128)(2,1)}, bf16[128,16,128]{0,2,1:T(8,128)(2,1)S(1)}, u32[]{:S(2)}) copy-start(bf16[128,16,128]{0,2,1:T(8,128)(2,1)S(1)} %get-tuple-element.168) | copy-start | bytes 1572868
  732.2 31.3 %copy-start.56 = (f32[128]{0:T(128)}, f32[128]{0:T(128)S(1)}, u32[]{:S(2)}) copy-start(f32[128]{0:T(128)S(1)} %get-tuple-element.170) | copy-start | bytes 1540
  732.3 31.3 %copy-start.54 = (f32[128]{0:T(128)}, f32[128]{0:T(128)S(1)}, u32[]{:S(2)}) copy-start(f32[128]{0:T(128)S(1)} %fusion.61) | copy-start | bytes 1540
  799.1 126.5 %all-to-all-start = ((bf16[24,53,2048]{2,1,0:T(8,128)(2,1)}), bf16[24,53,2048]{2,1,0:T(8,128)(2,1)}, u32[]{:S(2)}, u32[]{:S(2)}) async-start(bf16[24,53,2048]{2,1,0:T(8,128)(2,1)} %reshape.416), calls=%async_computation | async-start | bytes 11010048 | tf_op jit(solution)/shard_map/all_to_all | solution.py:166
  822.8 13.5 slice-start
  829.6 6.7 slice-start.1
  965.4 40.6 %copy-start.61 = (bf16[3,424,1024]{2,1,0:T(8,128)(2,1)}, bf16[3,424,1024]{2,1,0:T(8,128)(2,1)S(1)}, u32[]{:S(2)}) copy-start(bf16[3,424,1024]{2,1,0:T(8,128)(2,1)S(1)} %get-tuple-element.139) | copy-start | bytes 7815172
  1031.6 6.2 copy-start.63
  1031.6 158.9 %all-to-all-start.3 = ((bf16[3,424,2048]{2,0,1:T(4,128)(2,1)}), bf16[3,424,2048]{2,0,1:T(4,128)(2,1)}, u32[]{:S(2)}, u32[]{:S(2)}) async-start(bf16[3,424,2048]{2,0,1:T(4,128)(2,1)} %copy.185), calls=%async_computation.3 | async-start | bytes 13893632 | tf_op jit(solution)/shard_map/all_to_all | solution.py:225
  1061.7 133.6 %copy-start.45 = (f32[1,128,8]{1,2,0:T(8,128)S(1)}, f32[1,128,8]{1,2,0:T(8,128)}, u32[]{:S(2)}) copy-start(f32[1,128,8]{1,2,0:T(8,128)} %param.14) | copy-start | bytes 12292
  1190.5 156.6 %all-to-all-start.1 = ((bf16[3,424,2048]{2,0,1:T(4,128)(2,1)}), bf16[3,424,2048]{2,0,1:T(4,128)(2,1)}, u32[]{:S(2)}, u32[]{:S(2)}) async-start(bf16[3,424,2048]{2,0,1:T(4,128)(2,1)} %copy.180), calls=%async_computation.1 | async-start | bytes 13893632 | tf_op jit(solution)/shard_map/all_to_all | solution.py:224
  1195.3 240.8 %reduce-scatter.19.cloned.1.call-start = ((), (), s32[]{:S(2)}) async-start(), calls=%async_computation.20 | async-start | bytes 2621440
  1223.4 5.1 copy-start.7
  1223.4 5.1 copy-start.33
  1223.4 5.1 copy-start.55
  1223.4 5.5 copy-start.57
  1375.0 6.6 copy-start.20
  1393.7 6.3 copy-start.16
  1393.8 6.3 copy-start.18
  1406.4 9.6 copy-start.14
  1406.4 64.4 %reduce-scatter.13.cloned.1.call-start = ((), (), s32[]{:S(2)}) async-start(), calls=%async_computation.15 | async-start | bytes 2621440 | tf_op jit(solution)/shard_map/reduce_scatter | solution.py:278
  1415.5 634.5 %reduce-scatter.15.cloned.1.call-start = ((), (), s32[]{:S(2)}) async-start(), calls=%async_computation.16 | async-start | bytes 37748736 | tf_op jit(solution)/shard_map/reduce_scatter | solution.py:294
  1416.0 5.8 copy-start.10
  1416.0 5.7 copy-start.12
  1421.7 20.3 copy-start.26
  1421.7 20.3 copy-start.28
  1439.6 4.9 copy-start.35
  1439.6 4.9 copy-start.52
  1446.4 24.4 copy-start.9
  1446.4 24.4 copy-start.31
  1446.4 24.3 copy-start.48
  1506.5 607.7 %reduce-scatter.23.cloned.1.call-start = ((), (), s32[]{:S(2)}) async-start(), calls=%async_computation.22 | async-start | bytes 73728
  1506.8 12.4 copy-start.62
  1506.8 24.7 slice-start.2
  1519.2 12.3 slice-start.3
  1519.2 12.3 copy-start.64
  1531.5 10.9 copy-start.29
  1542.1 638.5 %reduce-scatter.21.cloned.1.call-start = ((), (), s32[]{:S(2)}) async-start(), calls=%async_computation.21 | async-start | bytes 1179648
  1558.4 885.4 %reduce-scatter.17.cloned.1.call-start = ((), (), s32[]{:S(2)}) async-start(), calls=%async_computation.18 | async-start | bytes 47185920 | tf_op jit(solution)/shard_map/reduce_scatter | solution.py:210
  1585.0 465.1 %copy-start.59 = (f32[128]{0:T(128)S(1)}, f32[128]{0:T(128)}, u32[]{:S(2)}) copy-start(f32[128]{0:T(128)} %copy-done.58) | copy-start | bytes 1540
  1585.0 465.1 %copy-start.24 = (f32[128,2048]{1,0:T(8,128)S(1)}, f32[128,2048]{1,0:T(8,128)}, u32[]{:S(2)}) copy-start(f32[128,2048]{1,0:T(8,128)} %get-tuple-element.172) | copy-start | bytes 3145732
  1585.0 946.7 %all-reduce.7.cloned.1.call-start = ((), (), s32[]{:S(2)}) async-start(), calls=%async_computation.17 | async-start | bytes 8388608 | tf_op jit(solution)/shard_map/psum | solution.py:307
  (25 other events, 71.0 us)
Sparse Core Ops, SparseCore 0:
  9.5 483.2 all-gather.8
  504.1 22.5 all-gather.18
  531.2 26.1 all-gather.10
  559.4 168.0 all-gather.12
  728.9 109.0 all-gather.14
  839.4 154.8 all-gather.16
  1406.5 29.5 reduce-scatter.18
  1439.3 31.3 reduce-scatter.12
  1506.7 543.3 reduce-scatter.14
  2053.9 60.2 reduce-scatter.22
  2118.2 62.3 reduce-scatter.20
  2183.3 260.4 reduce-scatter.16
  2446.2 85.4 all-reduce.6
